TPU v7x, 256 devices: a whole 4x4x8 slice. The times are simulated.
256 devices in a mesh: bal: 32 (over x, z), seq: 8 (over y, core).
Axes of the slice: x: 4, y: 4, z: 8, core: 2. Of those that a mesh axis runs over, the one named last changes fastest.
Arguments:
- tokens: bfloat16 [512, 64, 5120], P('bal', 'seq'), may hold values from -6 to 6
- w_qkv: bfloat16 [5120, 24, 384], P('bal', 'seq')
- q_gain: float32 [24, 128], P('seq')
- k_gain: float32 [24, 128], P('seq')
- modulation: float32 [32, 4, 2, 5120], P('bal'), may hold values from -3 to 3
- tile_owner: int32 [512], P('bal'), may hold values from 0 to 31, as said below
- clip_dims: int32 [32, 4, 3], P('bal'), may hold values from 0 to 4, as said below
Outputs:
- attn_out: bfloat16 [512, 64, 3072], P('bal', 'seq')
Inputs may be any that keep to these rules, and one draw needn't show every extreme that they name: `tile_owner`: each owner is named by exactly 16 tiles. The 16 tiles of one bal index name any owner at most 1 times, and in every draw some owner exactly 1 times. `clip_dims`: for each owner the clips' products f h w add up to 16; entries after its last clip are 0; a clip spans at most 2 tile frames, 3 tile rows and 4 tile columns and has 4 tiles or more.
All inputs are finite; a program needn't handle non-finite values.
Results may differ from a plain program's by a relative error of at most 0.006.
Values may be sent and summed in bfloat16 or wider, within the bound.
A program may use at most 128 MiB of HBM per device.

v0:
```python
import jax
import jax.numpy as jnp
from jax import lax
from jax.sharding import PartitionSpec as P

HEADS = 24
TILES_OWN = 16
eps_norm = 1e-06
score_fill = -1e30


def tile_layout(clip_shape):
    frames_of = clip_shape[:, 0]
    rows_of = clip_shape[:, 1]
    cols_of = clip_shape[:, 2]
    clip_sizes = frames_of * rows_of * cols_of
    clip_ends = jnp.cumsum(clip_sizes)
    clip_starts = clip_ends - clip_sizes
    local_index = jnp.arange(TILES_OWN, dtype=jnp.int32)
    member = jnp.sum((local_index[:, None] >= clip_ends[None, :]).astype(jnp.int32), axis=1)
    onehot = member[:, None] == jnp.arange(clip_shape.shape[0], dtype=jnp.int32)[None, :]

    def select_clip(values):
        return jnp.sum(jnp.where(onehot, values[None, :], 0), axis=1)

    offset = local_index - select_clip(clip_starts)
    height = jnp.maximum(select_clip(rows_of), 1)
    width_tiles = jnp.maximum(select_clip(cols_of), 1)
    frame_index = offset // (height * width_tiles)
    row_index = offset // width_tiles % height
    column = offset % width_tiles

    def within_one(coords):
        return jnp.abs(coords[:, None] - coords[None, :]) <= 1

    tile_mask = (
        (member[:, None] == member[None, :])
        & within_one(frame_index)
        & within_one(row_index)
        & within_one(column)
    )
    return (onehot, tile_mask)


def clip_rows(onehot, mod_table):
    picked = jnp.sum(jnp.where(onehot[:, :, None, None], mod_table[None], 0.0), axis=1)
    return (picked[:, 0], picked[:, 1])


def modulate(pieces, shift_rows, scale_rows):
    values = pieces.astype(jnp.float32)
    center = jnp.mean(values, axis=-1, keepdims=True)
    spread = jnp.mean(jnp.square(values - center), axis=-1, keepdims=True)
    normal = (values - center) * lax.rsqrt(spread + eps_norm)
    return (normal * (1.0 + scale_rows[:, None, :]) + shift_rows[:, None, :]).astype(jnp.bfloat16)


def attend(q_block, key_rows, values, block_mask):
    scores = jnp.einsum(
        "qhd,khd->hqk", q_block, key_rows, preferred_element_type=jnp.float32
    ) * key_rows.shape[2] ** (-0.5)
    scores = jnp.where(block_mask[None], scores, score_fill)
    largest = jnp.max(scores, axis=-1, keepdims=True)
    exp_scores = jnp.exp(scores - largest)
    totals = jnp.sum(exp_scores, axis=-1, keepdims=True)
    weights = (exp_scores / totals).astype(jnp.bfloat16)
    return jnp.einsum("hqk,khd->qhd", weights, values, preferred_element_type=jnp.float32)


def per_device(tokens, w_qkv, q_gain, k_gain, modulation, tile_owner, clip_dims):
    groups = lax.axis_size("bal")
    owned_tiles, piece_len, width_model = tokens.shape
    capacity = owned_tiles // min(groups, owned_tiles)
    slot_count = groups * capacity
    flat_weight = w_qkv.reshape(w_qkv.shape[0], -1)
    slot_ids = jnp.arange(slot_count, dtype=jnp.int32)
    earlier = jnp.arange(owned_tiles)[:, None] > jnp.arange(owned_tiles)[None, :]
    slot_rank = jnp.sum((tile_owner[:, None] == tile_owner[None, :]) & earlier, axis=1)
    target = tile_owner * capacity + slot_rank
    route_onehot = (slot_ids[:, None] == target[None, :]).astype(jnp.bfloat16)
    outbound = jnp.dot(
        route_onehot, tokens.reshape(owned_tiles, -1), preferred_element_type=jnp.float32
    ).astype(jnp.bfloat16)
    outbound = outbound.reshape(groups, capacity, piece_len, width_model)
    filled = jnp.sum(route_onehot, axis=1).reshape(groups, capacity)
    arrived, arrived_flags = (
        lax.all_to_all(outbound, "bal", split_axis=0, concat_axis=0, tiled=True),
        lax.all_to_all(filled, "bal", split_axis=0, concat_axis=0, tiled=True),
    )
    live_slots = arrived_flags.reshape(slot_count) > 0.5
    position = jnp.cumsum(live_slots.astype(jnp.int32)) - 1
    collect = ((jnp.arange(TILES_OWN)[:, None] == position[None, :]) & live_slots[None, :]).astype(
        jnp.bfloat16
    )
    compact = jnp.dot(
        collect, arrived.reshape(slot_count, -1), preferred_element_type=jnp.float32
    ).astype(jnp.bfloat16)
    compact = compact.reshape(TILES_OWN, piece_len, width_model)
    onehot, tile_mask = tile_layout(clip_dims[0])
    shift_rows, scale_rows = clip_rows(onehot, modulation[0])
    whole_tiles = lax.all_gather(compact, "seq", axis=1, tiled=True)
    normed = modulate(whole_tiles, shift_rows, scale_rows)
    tile_len = normed.shape[1]
    token_rows = normed.reshape(-1, width_model)
    total_tokens = token_rows.shape[0]
    per_dev_heads = q_gain.shape[0]
    projected = jnp.dot(
        token_rows,
        lax.all_gather(flat_weight, "bal", axis=0, tiled=True),
        preferred_element_type=jnp.float32,
    )
    projected = projected.reshape(total_tokens, per_dev_heads, 3, -1)
    query = projected[:, :, 0]
    keyed = projected[:, :, 1]
    valued = projected[:, :, 2].astype(jnp.bfloat16)
    sums_q, sums_k = lax.psum(
        (jnp.sum(jnp.square(query), axis=(1, 2)), jnp.sum(jnp.square(keyed), axis=(1, 2))), "seq"
    )
    features = HEADS * query.shape[2]
    q_normed = (
        query * lax.rsqrt(sums_q / features + eps_norm)[:, None, None] * q_gain[None]
    ).astype(jnp.bfloat16)
    k_normed = (
        keyed * lax.rsqrt(sums_k / features + eps_norm)[:, None, None] * k_gain[None]
    ).astype(jnp.bfloat16)
    token_mask = jnp.repeat(jnp.repeat(tile_mask, tile_len, axis=0), tile_len, axis=1)
    block_rows = min(512, total_tokens)
    outputs = []
    for block_start in range(0, total_tokens, block_rows):
        outputs.append(
            attend(
                q_normed[block_start : block_start + block_rows],
                k_normed,
                valued,
                token_mask[block_start : block_start + block_rows],
            )
        )
    attended = jnp.concatenate(outputs, axis=0).astype(jnp.bfloat16)
    head_major = attended.reshape(TILES_OWN, tile_len, -1)
    per_token = lax.all_to_all(head_major, "seq", split_axis=1, concat_axis=2, tiled=True)
    spread_back = jnp.dot(
        collect.T, per_token.reshape(TILES_OWN, -1), preferred_element_type=jnp.float32
    ).astype(jnp.bfloat16)
    spread_back = spread_back.reshape(groups, capacity, piece_len, -1)
    returned = lax.all_to_all(spread_back, "bal", split_axis=0, concat_axis=0, tiled=True)
    result = jnp.dot(
        route_onehot.T, returned.reshape(slot_count, -1), preferred_element_type=jnp.float32
    ).astype(jnp.bfloat16)
    return result.reshape(owned_tiles, piece_len, -1)


def solution(mesh):
    return jax.shard_map(
        per_device,
        mesh=mesh,
        in_specs=(
            P("bal", "seq", None),
            P("bal", "seq", None),
            P("seq", None),
            P("seq", None),
            P("bal", None, None, None),
            P("bal"),
            P("bal", None, None),
        ),
        out_specs=P("bal", "seq", None),
        check_vma=False,
    )
```

profile of v0, /device:TPU:32, one launch (start us, length us, event | category | flops | bytes accessed | tf_op | source)
XLA Modules:
  0.0 369.4 jit_solution(7702107884539255839)
XLA Ops:
  6.5 1.8 copy.85
  8.3 0.9 convert_reduce_fusion.1
  9.2 0.7 add.87
  9.9 0.1 fusion.52
  10.0 0.7 copy.60
  10.7 11.2 %all-to-all-start = ((bf16[32,1,1]{2,1,0:T(2,128)(2,1)}), bf16[32,1,1]{2,1,0:T(2,128)(2,1)S(1)}, u32[]{:S(2)}, u32[]{:S(2)}) async-start(bf16[32,1,1]{2,1,0:T(2,128)(2,1)} %copy.60), calls=%async_computation | async-start | bytes 32768 | tf_op jit(solution)/shard_map/all_to_all | solution.py:88
  21.9 2.0 copy.86
  23.9 0.9 convolution_convert_fusion
  24.9 3.0 copy.87
  27.9 2.6 all-to-all-done
  30.5 7.2 %all-to-all-start.1 = ((bf16[32,1,8,5120]{3,2,1,0:T(8,128)(2,1)}), bf16[32,1,8,5120]{3,2,1,0:T(8,128)(2,1)S(1)}, u32[]{:S(2)}, u32[]{:S(2)}) async-start(bf16[32,1,8,5120]{3,2,1,0:T(8,128)(2,1)} %bitcast.2), calls=%async_computation.1 | async-start | bytes 5242880 | tf_op jit(solution)/shard_map/all_to_all | solution.py:87
  37.7 0.2 all-gather.3.cloned.1.call-start
  37.9 0.7 compare_reduce_fusion
  38.7 0.1 add_reduce_fusion
  38.8 76.5 %all-to-all-done.1 = bf16[32,1,8,5120]{3,2,1,0:T(8,128)(2,1)S(1)} async-done(((bf16[32,1,8,5120]{3,2,1,0:T(8,128)(2,1)}), bf16[32,1,8,5120]{3,2,1,0:T(8,128)(2,1)S(1)}, u32[]{:S(2)}, u32[]{:S(2)}) %all-to-all-start.1) | async-done | bytes 2621472 | tf_op jit(solution)/shard_map/all_to_all | solution.py:87
  115.3 1.4 copy.88
  116.8 0.5 convolution_convert_fusion.1
  117.3 1.8 copy.89
  119.1 0.1 copy.63
  119.2 0.2 slice_reduce_fusion.1
  119.4 0.1 reduce.3
  119.5 0.1 convert_reduce_fusion.2
  119.6 0.1 select_reduce_fusion.2
  119.7 0.2 and_select_fusion.3
  120.0 0.1 fusion.47
  120.1 0.1 fusion.63
  120.1 0.1 broadcast_in_dim.121
  120.2 0.1 slice.56
  120.3 0.1 broadcast_in_dim.122
  120.5 0.9 copy.66
  121.4 0.1 broadcast_in_dim.126
  121.5 0.1 slice.61
  121.6 0.1 broadcast_in_dim.127
  121.8 0.9 copy.69
  122.8 0.3 select_reduce_fusion
  123.1 36.1 %all-gather.5.cloned.1.call-done = bf16[5120,1152]{1,0:T(8,128)(2,1)} async-done(((bf16[160,1152]{1,0:T(8,128)(2,1)}), bf16[5120,1152]{1,0:T(8,128)(2,1)}) %all-gather.5.cloned.1.call-update) | async-done | bytes 11796496 | tf_op jit(solution)/shard_map/all_gather | solution.py:109
  159.2 15.2 %copy.65 = bf16[1152,5120]{1,0:T(8,128)(2,1)} copy(bf16[1152,5120]{0,1:T(8,128)(2,1)} %bitcast.85) | data formatting | bytes 23592960 | tf_op jit(solution)/shard_map/dot_general | solution.py:107
  174.3 47.2 %all-gather.3.cloned.1.call-done = bf16[16,64,5120]{2,1,0:T(8,128)(2,1)} async-done(((bf16[16,8,5120]{2,1,0:T(8,128)(2,1)}), bf16[16,64,5120]{2,1,0:T(8,128)(2,1)}) %all-gather.3.cloned.1.call-update) | async-done | bytes 10485776 | tf_op jit(solution)/shard_map/all_gather | solution.py:101
  221.6 5.6 %convert_reduce_fusion = f32[16,64]{1,0:T(8,128)S(1)} fusion(bf16[16,64,5120]{2,1,0:T(8,128)(2,1)} %all-gather.3.cloned.1.call-done), kind=kLoop, calls=%fused_computation.7 | loop fusion | flops 10484736 | bytes 10489856 | tf_op jit(solution)/shard_map/reduce_sum | solution.py:52
  227.2 1.3 copy-done
  228.5 2.8 fusion.4
  231.4 6.7 %fusion.7 = bf16[16,64,5120]{2,1,0:T(8,128)(2,1)S(1)} fusion(bf16[16,64,5120]{2,1,0:T(8,128)(2,1)S(1)} %copy-done, f32[16,5120]{1,0:T(8,128)S(1)} %get-tuple-element.18, f32[16,5120]{1,0:T(8,128)S(1)} %get-tuple-element.17, f32[16,64]{1,0:T(8,128)S(1)} %add_rsqrt_fusion, f32[16,64]{1,0:T(8,128)S(1)} %broadcast_multiply_fusion), kind=kLoop, calls=%fused_computation.13 | loop fusion | flops 31457280 | bytes 21635072 | tf_op jit(solution)/shard_map/convert_element_type | solution.py:55
  238.1 15.5 %fusion.74 = f32[1024,3,3,128]{0,3,2,1:T(8,128)S(1)} fusion(bf16[1024,5120,1,1]{1,0,3,2:T(8,128)(2,1)S(1)} %bitcast.87, bf16[3,3,128,5120]{3,2,1,0:T(8,128)(2,1)} %bitcast.86), kind=kOutput, calls=%fused_computation.108 | convolution fusion | flops 12079595520 | bytes 27000832 | tf_op jit(solution)/shard_map/dot_general | solution.py:107
  253.7 2.1 copy-done.1
  255.8 0.3 multiply_reduce_fusion.1
  256.1 13.6 %all-reduce = (f32[1024]{0:T(1024)S(1)}, f32[1024]{0:T(1024)S(1)}) all-reduce(f32[1024]{0:T(1024)S(1)} %get-tuple-element.6, f32[1024]{0:T(1024)S(1)} %get-tuple-element.5), channel_id=1, replica_groups=mesh['bal'=32,'seq'=8] {'seq'}, use_global_device_ids=true, to_apply=%region_14.15 | all-reduce | flops 2048 | bytes 16384 | tf_op jit(solution)/shard_map/psum | solution.py:116
  269.7 2.2 multiply_convert_fusion.1
  272.0 5.1 %fusion.69 = (f32[3,512]{1,0:T(4,128)S(1)}, f32[3,512,1024]{2,1,0:T(8,128)}) fusion(pred[512,1024]{1,0:T(8,128)(4,1)S(1)} %copy.66, bf16[1024,3,128]{0,2,1:T(8,128)(2,1)S(1)} %get-tuple-element.16, bf16[1024,3,128]{0,2,1:T(8,128)(2,1)S(1)} %get-tuple-element.15), kind=kOutput, calls=%fused_computation.107 | convolution fusion | flops 408945664 | bytes 8001536 | tf_op jit(solution)/shard_map/sub | solution.py:64
  277.0 5.1 %fusion.64 = (f32[3,512]{1,0:T(4,128)S(1)}, f32[3,512,1024]{2,1,0:T(8,128)}) fusion(pred[512,1024]{1,0:T(8,128)(4,1)S(1)} %copy.69, bf16[1024,3,128]{0,2,1:T(8,128)(2,1)S(1)} %get-tuple-element.16, bf16[1024,3,128]{0,2,1:T(8,128)(2,1)S(1)} %get-tuple-element.15), kind=kOutput, calls=%fused_computation.106 | convolution fusion | flops 408945664 | bytes 8001536 | tf_op jit(solution)/shard_map/sub | solution.py:64
  282.1 4.7 %fusion.20 = bf16[512,3,128]{0,2,1:T(8,128)(2,1)S(1)} fusion(f32[3,512,1024]{2,1,0:T(8,128)} %get-tuple-element.30, f32[3,512]{1,0:T(4,128)S(1)} %get-tuple-element.29, f32[1024,3,3,128]{0,3,2,1:T(8,128)} %copy-done.1), kind=kOutput, calls=%fused_computation.40 | convolution fusion | flops 405995520 | bytes 7477248 | tf_op jit(solution)/shard_map/hqk,khd->qhd/dot_general | solution.py:67
  286.8 0.4 copy-done.6
  287.1 2.7 fusion.21
  289.8 0.1 pad_maximum_fusion
  289.9 1.0 reshape.312
  290.9 1.4 copy.73
  292.3 15.7 %all_to_all.34 = bf16[16,64,384]{2,0,1:T(8,128)(2,1)S(1)} all-to-all(bf16[16,64,384]{2,0,1:T(8,128)(2,1)S(1)} %copy.73), channel_id=1, replica_groups=mesh['bal'=32,'seq'=8] {'seq'}, dimensions={1} | all-to-all | bytes 1572864 | tf_op jit(solution)/shard_map/all_to_all | solution.py:140
  308.0 0.5 copy.75
  308.5 0.5 copy.90
  308.9 0.6 convolution_convert_fusion.2
  309.5 0.9 copy.91
  310.4 49.6 %all_to_all.35 = bf16[32,1,8,3072]{3,2,1,0:T(8,128)(2,1)S(1)} all-to-all(bf16[32,1,8,3072]{3,2,1,0:T(8,128)(2,1)S(1)} %bitcast.93), channel_id=1, replica_groups=mesh['bal'=32,'seq'=8] {'bal'}, dimensions={0} | all-to-all | bytes 3145728 | tf_op jit(solution)/shard_map/all_to_all | solution.py:145
  360.0 0.9 copy.92
  360.9 0.4 convolution_convert_fusion.3
  361.3 1.3 copy.93
  (22 shorter events, 0.2 us)
Async XLA Ops:
  6.5 152.6 %all-gather.5.cloned.1.call-start = ((), (), s32[]{:S(2)}) async-start(), calls=%async_computation.5 | async-start | bytes 12165120 | tf_op jit(solution)/shard_map/all_gather | solution.py:109
  10.7 19.8 %all-to-all-start = ((bf16[32,1,1]{2,1,0:T(2,128)(2,1)}), bf16[32,1,1]{2,1,0:T(2,128)(2,1)S(1)}, u32[]{:S(2)}, u32[]{:S(2)}) async-start(bf16[32,1,1]{2,1,0:T(2,128)(2,1)} %copy.60), calls=%async_computation | async-start | bytes 32768 | tf_op jit(solution)/shard_map/all_to_all | solution.py:88
  30.5 84.8 %all-to-all-start.1 = ((bf16[32,1,8,5120]{3,2,1,0:T(8,128)(2,1)}), bf16[32,1,8,5120]{3,2,1,0:T(8,128)(2,1)S(1)}, u32[]{:S(2)}, u32[]{:S(2)}) async-start(bf16[32,1,8,5120]{3,2,1,0:T(8,128)(2,1)} %bitcast.2), calls=%async_computation.1 | async-start | bytes 5242880 | tf_op jit(solution)/shard_map/all_to_all | solution.py:87
  37.7 183.9 %all-gather.3.cloned.1.call-start = ((), (), s32[]{:S(2)}) async-start(), calls=%async_computation.4 | async-start | bytes 11796480 | tf_op jit(solution)/shard_map/all_gather | solution.py:101
  116.7 2.3 copy-start.5
  116.8 6.0 %copy-start.2 = (f32[1,4,2,5120]{3,2,1,0:T(2,128)S(1)}, f32[1,4,2,5120]{3,2,1,0:T(2,128)}, u32[]{:S(2)}) copy-start(f32[1,4,2,5120]{3,2,1,0:T(2,128)} %param.11) | copy-start | bytes 491524
  221.6 7.0 %copy-start = (bf16[16,64,5120]{2,1,0:T(8,128)(2,1)S(1)}, bf16[16,64,5120]{2,1,0:T(8,128)(2,1)}, u32[]{:S(2)}) copy-start(bf16[16,64,5120]{2,1,0:T(8,128)(2,1)} %all-gather.3.cloned.1.call-done) | copy-start | bytes 31457284
  238.1 31.6 %copy-start.3 = (f32[3,128]{1,0:T(4,128)S(1)}, f32[3,128]{1,0:T(4,128)}, u32[]{:S(2)}) copy-start(f32[3,128]{1,0:T(4,128)} %param.9) | copy-start | bytes 4612
  238.1 31.6 %copy-start.4 = (f32[3,128]{1,0:T(4,128)S(1)}, f32[3,128]{1,0:T(4,128)}, u32[]{:S(2)}) copy-start(f32[3,128]{1,0:T(4,128)} %param.10) | copy-start | bytes 4612
  253.7 2.1 copy-start.1
  282.1 5.0 %copy-start.6 = (f32[3,512,1024]{2,1,0:T(8,128)S(1)}, f32[3,512,1024]{2,1,0:T(8,128)}, u32[]{:S(2)}) copy-start(f32[3,512,1024]{2,1,0:T(8,128)} %get-tuple-element.28) | copy-start | bytes 18874372
Sparse Core Ops, SparseCore 0:
  9.9 149.1 all-gather.4
  161.0 60.5 all-gather.2
where the time goes:
time: 370 us; the launch traced here: 369 us
  waiting for transfers between devices  162 us (44%)
  blocking collectives  78.9 us (21%)
  local copies, waits for them, and re-layouts  38.9 us (11%)
  matrix products  35.4 us (10%)
  other arithmetic  21.5 us (6%)
  starting transfers between devices  18.6 us (5%)
  between operations  13.7 us (4%)
    all_to_all x1, waiting for transfers between devices, per_device(): lax.all_to_all(outbound, 'bal', split_axis=0, concat_axis=0, tiled=True)  76.5 us
    all_to_all x1, blocking collectives, per_device(): lax.all_to_all(spread_back, 'bal', split_axis=0, concat_axis=0, tiled=True)  49.6 us
    all_gather x1, waiting for transfers between devices, per_device(): whole_tiles = lax.all_gather(compact, 'seq', axis=1, tiled=True)  47.2 us
    all_gather x1, waiting for transfers between devices, per_device(): lax.all_gather(flat_weight, 'bal', axis=0, tiled=True)  36.1 us
    unnamed x23, local copies, waits for them, and re-layouts  15.7 us
    all_to_all x1, blocking collectives, per_device(): lax.all_to_all(head_major, 'seq', split_axis=1, concat_axis=2, tiled=True)  15.7 us
    dot_general x1, matrix products, per_device(): jnp.dot(token_rows, lax.all_gather(flat_weight, 'bal', axis=0, tiled=True...  15.5 us
    dot_general x1, local copies, waits for them, and re-layouts, per_device(): jnp.dot(token_rows, lax.all_gather(flat_weight, 'bal', axis=0, tiled=True...  15.2 us
  transfers between devices with their start and end apart: 4, of which 4 were waited for; matrix products, arithmetic and copies ran while one was open for 9% of the time, Pallas kernels for 0%

commit v1 on v0

--- a/solution.py
+++ b/solution.py
@@ -98,7 +98,9 @@
     compact = compact.reshape(TILES_OWN, piece_len, width_model)
     onehot, tile_mask = tile_layout(clip_dims[0])
     shift_rows, scale_rows = clip_rows(onehot, modulation[0])
-    whole_tiles = lax.all_gather(compact, "seq", axis=1, tiled=True)
+    whole_tiles = jnp.concatenate(
+        lax.all_to_all(jnp.stack([compact] * lax.axis_size("seq")), "seq", 0, 0), axis=1
+    )
     normed = modulate(whole_tiles, shift_rows, scale_rows)
     tile_len = normed.shape[1]
     token_rows = normed.reshape(-1, width_model)

time: 370 us -> 415 us (1.12)
  waiting for transfers between devices: 162 us -> 192 us
  other arithmetic: 21.5 us -> 30.5 us
  starting transfers between devices: 18.6 us -> 23.9 us
  blocking collectives: 78.9 us -> 73.8 us
    all_to_all x0 -> x1, waiting for transfers between devices: none -> 113 us  [per_device(): lax.all_to_all(jnp.stack([compact] * lax.axis_size('seq')), 'seq', 0, 0)]
    all_gather x1 -> x0, waiting for transfers between devices: 47.2 us -> none  [per_device(): whole_tiles = lax.all_gather(compact, 'seq', axis=1, tiled=True)]
    all_gather x1, waiting for transfers between devices: 36.1 us -> 0.01 us  [per_device(): lax.all_gather(flat_weight, 'bal', axis=0, tiled=True)]
    all_to_all x0 -> x1, starting transfers between devices: none -> 5.55 us  [per_device(): lax.all_to_all(jnp.stack([compact] * lax.axis_size('seq')), 'seq', 0, 0)]
    another operation x0 -> x1, local copies, waits for them, and re-layouts: none -> 5.25 us  [per_device(): jnp.stack([compact] * lax.axis_size('seq'))]
    convert_element_type x1, other arithmetic: 6.73 us -> 11.9 us  [modulate(): (normal * (1.0 + scale_rows[:, None, :]) + shift_rows[:, None, :]).astype...]
    all_to_all x1, blocking collectives: 49.6 us -> 45.1 us  [per_device(): lax.all_to_all(spread_back, 'bal', split_axis=0, concat_axis=0, tiled=True)]
    unnamed x23 -> x21, local copies, waits for them, and re-layouts: 15.7 us -> 13.3 us
  transfers between devices with their start and end apart: 4 -> 4, of which waited for: 4 -> 3; matrix products, arithmetic and copies ran while one was open for 9% -> 11% of each run, Pallas kernels for 0% -> 0%
where the time goes in v1:
time: 415 us; the launch traced here: 414 us
  waiting for transfers between devices  192 us (46%)
  blocking collectives  73.8 us (18%)
  local copies, waits for them, and re-layouts  42.3 us (10%)
  matrix products  37.3 us (9%)
  other arithmetic  30.5 us (7%)
  starting transfers between devices  23.9 us (6%)
  between operations  13.7 us (3%)
    all_to_all x1, waiting for transfers between devices, per_device(): lax.all_to_all(jnp.stack([compact] * lax.axis_size('seq')), 'seq', 0, 0)  113 us
    all_to_all x1, waiting for transfers between devices, per_device(): lax.all_to_all(outbound, 'bal', split_axis=0, concat_axis=0, tiled=True)  76.8 us
    all_to_all x1, blocking collectives, per_device(): lax.all_to_all(spread_back, 'bal', split_axis=0, concat_axis=0, tiled=True)  45.1 us
    dot_general x1, matrix products, per_device(): jnp.dot(token_rows, lax.all_gather(flat_weight, 'bal', axis=0, tiled=True...  17.5 us
    all_to_all x1, blocking collectives, per_device(): lax.all_to_all(head_major, 'seq', split_axis=1, concat_axis=2, tiled=True)  15.7 us
    dot_general x1, local copies, waits for them, and re-layouts, per_device(): jnp.dot(token_rows, lax.all_gather(flat_weight, 'bal', axis=0, tiled=True...  15.1 us
    unnamed x21, local copies, waits for them, and re-layouts  13.3 us
    psum x1, blocking collectives, per_device(): lax.psum((jnp.sum(jnp.square(query), axis=(1, 2)), jnp.sum(jnp.square(key...  13.1 us
  transfers between devices with their start and end apart: 4, of which 3 were waited for; matrix products, arithmetic and copies ran while one was open for 11% of the time, Pallas kernels for 0%

profile of v1, /device:TPU:32, one launch (start us, length us, event | category | flops | bytes accessed | tf_op | source)
XLA Modules:
  0.0 413.8 jit_solution(7536700169911304474)
XLA Ops:
  6.5 1.8 copy.128
  8.3 0.9 convert_reduce_fusion
  9.2 0.7 add.96
  9.9 0.1 fusion.55
  10.0 0.7 copy.97
  10.7 11.2 %all-to-all-start = ((bf16[32,1,1]{2,1,0:T(2,128)(2,1)}), bf16[32,1,1]{2,1,0:T(2,128)(2,1)S(1)}, u32[]{:S(2)}, u32[]{:S(2)}) async-start(bf16[32,1,1]{2,1,0:T(2,128)(2,1)} %copy.97), calls=%async_computation | async-start | bytes 32768 | tf_op jit(solution)/shard_map/all_to_all | solution.py:88
  21.9 2.0 copy.129
  23.9 0.9 convolution_convert_fusion
  24.9 3.0 copy.130
  27.9 2.6 all-to-all-done
  30.5 7.2 %all-to-all-start.1 = ((bf16[32,1,8,5120]{3,2,1,0:T(8,128)(2,1)}), bf16[32,1,8,5120]{3,2,1,0:T(8,128)(2,1)S(1)}, u32[]{:S(2)}, u32[]{:S(2)}) async-start(bf16[32,1,8,5120]{3,2,1,0:T(8,128)(2,1)} %bitcast.2), calls=%async_computation.1 | async-start | bytes 5242880 | tf_op jit(solution)/shard_map/all_to_all | solution.py:87
  37.7 0.7 compare_reduce_fusion
  38.4 0.1 add_reduce_fusion
  38.5 76.8 %all-to-all-done.1 = bf16[32,1,8,5120]{3,2,1,0:T(8,128)(2,1)S(1)} async-done(((bf16[32,1,8,5120]{3,2,1,0:T(8,128)(2,1)}), bf16[32,1,8,5120]{3,2,1,0:T(8,128)(2,1)S(1)}, u32[]{:S(2)}, u32[]{:S(2)}) %all-to-all-start.1) | async-done | bytes 2621472 | tf_op jit(solution)/shard_map/all_to_all | solution.py:87
  115.3 1.4 copy.131
  116.7 0.5 convolution_convert_fusion.1
  117.2 0.7 copy.132
  118.0 5.2 %stack.3 = bf16[8,16,8,5120]{3,2,1,0:T(8,128)(2,1)} broadcast(bf16[16,8,5120]{2,1,0:T(8,128)(2,1)S(1)} %bitcast.124), dimensions={1,2,3} | broadcast | bytes 11796480 | tf_op jit(solution)/shard_map/stack | solution.py:102
  123.2 5.6 %all-to-all-start.2 = ((bf16[8,16,8,5120]{3,2,1,0:T(8,128)(2,1)}), bf16[8,16,8,5120]{3,2,1,0:T(8,128)(2,1)}, u32[]{:S(2)}, u32[]{:S(2)}) async-start(bf16[8,16,8,5120]{3,2,1,0:T(8,128)(2,1)} %stack.3), calls=%async_computation.2 | async-start | bytes 20971520 | tf_op jit(solution)/shard_map/all_to_all | solution.py:102
  128.8 0.1 copy.106
  128.9 0.2 slice_reduce_fusion.1
  129.1 0.1 reduce.5
  129.3 0.1 convert_reduce_fusion.1
  129.4 0.1 select_reduce_fusion.2
  129.5 0.2 and_select_fusion.3
  129.9 0.1 broadcast_in_dim.121
  130.0 0.1 slice.56
  130.1 0.1 broadcast_in_dim.122
  130.2 0.9 copy.109
  131.2 0.1 broadcast_in_dim.126
  131.2 0.1 slice.61
  131.4 0.1 broadcast_in_dim.127
  131.5 0.9 copy.112
  132.5 0.3 select_reduce_fusion
  132.8 112.9 %all-to-all-done.2 = bf16[8,16,8,5120]{3,2,1,0:T(8,128)(2,1)} async-done(((bf16[8,16,8,5120]{3,2,1,0:T(8,128)(2,1)}), bf16[8,16,8,5120]{3,2,1,0:T(8,128)(2,1)}, u32[]{:S(2)}, u32[]{:S(2)}) %all-to-all-start.2) | async-done | bytes 10485792 | tf_op jit(solution)/shard_map/all_to_all | solution.py:102
  245.7 5.4 %fusion.2 = f32[16,8,8]{2,1,0:T(8,128)S(1)} fusion(bf16[8,16,8,5120]{3,2,1,0:T(8,128)(2,1)} %all-to-all-done.2), kind=kLoop, calls=%fused_computation.8 | loop fusion | flops 10484736 | bytes 10489856 | tf_op jit(solution)/shard_map/reduce_sum | solution.py:52
  251.1 0.1 copy.101
  251.2 0.1 copy.103
  251.3 6.8 %fusion.5 = f32[16,8,8]{2,1,0:T(8,128)S(1)} fusion(f32[16,8,8]{2,1,0:T(8,128)S(1)} %copy.103, bf16[8,16,8,5120]{3,2,1,0:T(8,128)(2,1)} %all-to-all-done.2), kind=kLoop, calls=%fused_computation.11 | loop fusion | flops 20970496 | bytes 10493952 | tf_op jit(solution)/shard_map/reduce_sum | solution.py:53
  258.1 0.1 copy.104
  258.4 11.9 %fusion.10 = bf16[16,64,5120]{2,1,0:T(8,128)(2,1)} fusion(f32[16,5120]{1,0:T(8,128)S(1)} %get-tuple-element.18, f32[16,5120]{1,0:T(8,128)S(1)} %get-tuple-element.17, f32[16,64]{1,0:T(8,128)S(1)} %copy.105, f32[16,64]{1,0:T(8,128)S(1)} %copy.102, bf16[8,16,8,5120]{3,2,1,0:T(8,128)(2,1)} %all-to-all-done.2), kind=kLoop, calls=%fused_computation.16 | loop fusion | flops 31457280 | bytes 21635072 | tf_op jit(solution)/shard_map/convert_element_type | solution.py:55
  270.2 15.1 %copy.108 = bf16[1152,5120]{1,0:T(8,128)(2,1)} copy(bf16[1152,5120]{0,1:T(8,128)(2,1)} %bitcast.112) | data formatting | bytes 23592960 | tf_op jit(solution)/shard_map/dot_general | solution.py:109
  285.4 17.5 %fusion.78 = f32[1024,3,3,128]{0,3,2,1:T(8,128)S(1)} fusion(bf16[1024,5120,1,1]{1,0,3,2:T(8,128)(2,1)} %bitcast.114, bf16[3,3,128,5120]{3,2,1,0:T(8,128)(2,1)} %bitcast.113), kind=kOutput, calls=%fused_computation.112 | convolution fusion | flops 12079595520 | bytes 27000832 | tf_op jit(solution)/shard_map/dot_general | solution.py:109
  302.8 2.1 copy-done
  304.9 0.3 multiply_reduce_fusion.1
  305.2 13.1 %all-reduce = (f32[1024]{0:T(1024)S(1)}, f32[1024]{0:T(1024)S(1)}) all-reduce(f32[1024]{0:T(1024)S(1)} %get-tuple-element.6, f32[1024]{0:T(1024)S(1)} %get-tuple-element.5), channel_id=1, replica_groups=mesh['bal'=32,'seq'=8] {'seq'}, use_global_device_ids=true, to_apply=%region_14.15 | all-reduce | flops 2048 | bytes 16384 | tf_op jit(solution)/shard_map/psum | solution.py:118
  318.3 2.2 multiply_convert_fusion.1
  320.6 5.1 %fusion.73 = (f32[3,512]{1,0:T(4,128)S(1)}, f32[3,512,1024]{2,1,0:T(8,128)}) fusion(pred[512,1024]{1,0:T(8,128)(4,1)S(1)} %copy.109, bf16[1024,3,128]{0,2,1:T(8,128)(2,1)S(1)} %get-tuple-element.16, bf16[1024,3,128]{0,2,1:T(8,128)(2,1)S(1)} %get-tuple-element.15), kind=kOutput, calls=%fused_computation.111 | convolution fusion | flops 408945664 | bytes 8001536 | tf_op jit(solution)/shard_map/sub | solution.py:64
  325.6 5.1 %fusion.68 = (f32[3,512]{1,0:T(4,128)S(1)}, f32[3,512,1024]{2,1,0:T(8,128)}) fusion(pred[512,1024]{1,0:T(8,128)(4,1)S(1)} %copy.112, bf16[1024,3,128]{0,2,1:T(8,128)(2,1)S(1)} %get-tuple-element.16, bf16[1024,3,128]{0,2,1:T(8,128)(2,1)S(1)} %get-tuple-element.15), kind=kOutput, calls=%fused_computation.110 | convolution fusion | flops 408945664 | bytes 8001536 | tf_op jit(solution)/shard_map/sub | solution.py:64
  330.7 4.7 %fusion.23 = bf16[512,3,128]{0,2,1:T(8,128)(2,1)S(1)} fusion(f32[3,512,1024]{2,1,0:T(8,128)} %get-tuple-element.32, f32[3,512]{1,0:T(4,128)S(1)} %get-tuple-element.31, f32[1024,3,3,128]{0,3,2,1:T(8,128)} %copy-done), kind=kOutput, calls=%fused_computation.43 | convolution fusion | flops 405995520 | bytes 7477248 | tf_op jit(solution)/shard_map/hqk,khd->qhd/dot_general | solution.py:67
  335.4 0.4 copy-done.5
  335.7 2.7 fusion.24
  338.4 0.1 pad_maximum_fusion
  338.5 1.3 reshape.399
  339.8 1.4 copy.116
  341.2 15.7 %all_to_all.39 = bf16[16,64,384]{2,0,1:T(8,128)(2,1)S(1)} all-to-all(bf16[16,64,384]{2,0,1:T(8,128)(2,1)S(1)} %copy.116), channel_id=1, replica_groups=mesh['bal'=32,'seq'=8] {'seq'}, dimensions={1} | all-to-all | bytes 1572864 | tf_op jit(solution)/shard_map/all_to_all | solution.py:142
  356.9 0.5 copy.118
  357.3 0.5 copy.133
  357.8 0.6 convolution_convert_fusion.2
  358.4 0.9 copy.134
  359.3 45.1 %all_to_all.40 = bf16[32,1,8,3072]{3,2,1,0:T(8,128)(2,1)S(1)} all-to-all(bf16[32,1,8,3072]{3,2,1,0:T(8,128)(2,1)S(1)} %bitcast.120), channel_id=1, replica_groups=mesh['bal'=32,'seq'=8] {'bal'}, dimensions={0} | all-to-all | bytes 3145728 | tf_op jit(solution)/shard_map/all_to_all | solution.py:147
  404.3 0.9 copy.135
  405.2 0.4 convolution_convert_fusion.3
  405.6 1.3 copy.136
  (25 shorter events, 0.5 us)
Async XLA Ops:
  6.5 263.7 %all-gather.2.cloned.1.call-start = ((), (), s32[]{:S(2)}) async-start(), calls=%async_computation.5 | async-start | bytes 12165120 | tf_op jit(solution)/shard_map/all_gather | solution.py:111
  10.7 19.8 %all-to-all-start = ((bf16[32,1,1]{2,1,0:T(2,128)(2,1)}), bf16[32,1,1]{2,1,0:T(2,128)(2,1)S(1)}, u32[]{:S(2)}, u32[]{:S(2)}) async-start(bf16[32,1,1]{2,1,0:T(2,128)(2,1)} %copy.97), calls=%async_computation | async-start | bytes 32768 | tf_op jit(solution)/shard_map/all_to_all | solution.py:88
  30.5 84.8 %all-to-all-start.1 = ((bf16[32,1,8,5120]{3,2,1,0:T(8,128)(2,1)}), bf16[32,1,8,5120]{3,2,1,0:T(8,128)(2,1)S(1)}, u32[]{:S(2)}, u32[]{:S(2)}) async-start(bf16[32,1,8,5120]{3,2,1,0:T(8,128)(2,1)} %bitcast.2), calls=%async_computation.1 | async-start | bytes 5242880 | tf_op jit(solution)/shard_map/all_to_all | solution.py:87
  123.2 5.6 %copy-start.4 = (s32[1,4,3]{1,0,2:T(1,128)S(1)}, s32[1,4,3]{1,0,2:T(1,128)}, u32[]{:S(2)}) copy-start(s32[1,4,3]{1,0,2:T(1,128)} %param.13) | copy-start | bytes 148
  123.2 9.2 %copy-start.1 = (f32[1,4,2,5120]{3,2,1,0:T(2,128)S(1)}, f32[1,4,2,5120]{3,2,1,0:T(2,128)}, u32[]{:S(2)}) copy-start(f32[1,4,2,5120]{3,2,1,0:T(2,128)} %param.11) | copy-start | bytes 491524
  123.2 122.5 %all-to-all-start.2 = ((bf16[8,16,8,5120]{3,2,1,0:T(8,128)(2,1)}), bf16[8,16,8,5120]{3,2,1,0:T(8,128)(2,1)}, u32[]{:S(2)}, u32[]{:S(2)}) async-start(bf16[8,16,8,5120]{3,2,1,0:T(8,128)(2,1)} %stack.3), calls=%async_computation.2 | async-start | bytes 20971520 | tf_op jit(solution)/shard_map/all_to_all | solution.py:102
  285.3 33.0 %copy-start.2 = (f32[3,128]{1,0:T(4,128)S(1)}, f32[3,128]{1,0:T(4,128)}, u32[]{:S(2)}) copy-start(f32[3,128]{1,0:T(4,128)} %param.9) | copy-start | bytes 4612
  285.4 33.0 %copy-start.3 = (f32[3,128]{1,0:T(4,128)S(1)}, f32[3,128]{1,0:T(4,128)}, u32[]{:S(2)}) copy-start(f32[3,128]{1,0:T(4,128)} %param.10) | copy-start | bytes 4612
  302.8 2.1 copy-start
  330.7 5.0 %copy-start.5 = (f32[3,512,1024]{2,1,0:T(8,128)S(1)}, f32[3,512,1024]{2,1,0:T(8,128)}, u32[]{:S(2)}) copy-start(f32[3,512,1024]{2,1,0:T(8,128)} %get-tuple-element.30) | copy-start | bytes 18874372
Sparse Core Ops, SparseCore 0:
  9.9 149.1 all-gather.1
